TPU v7x, 256 devices: a whole 4x4x8 slice. The times are simulated.
256 devices in a mesh: section: 8 (over y, z_hi), dp: 32 (over z_lo, x, core).
Axes of the slice: x: 4, y: 4, z: 8 (z_hi: 2, z_lo: 4; z = z_hi * 4 + z_lo), core: 2. Of those that a mesh axis runs over, the one named last changes fastest.
Arguments:
- inputs: bfloat16 [4, 2048, 2048], P(None, 'dp'), may hold values from -6 to 6
- cotangent: bfloat16 [4, 2048, 2048], P(None, 'dp'), may hold values from -6 to 6
- weight: bfloat16 [8, 2048, 2048], P('section'), may hold values from -0.125 to 0.125
- factor_old: float32 [8, 2048, 2048], P('section', 'dp'), may hold values from -1.5 to 3.5, as said below
- stale_inverse: bfloat16 [8, 2048, 2048], P('section', 'dp'), may hold values from -0.5 to 0.75, as said below
Outputs:
- input_grads: bfloat16 [8, 4, 2048, 2048], P('section', None, 'dp')
- factor_new: float32 [8, 2048, 2048], P('section', 'dp')
- inverse_new: bfloat16 [8, 2048, 2048], P('section', 'dp')
Inputs may be any that keep to these rules, and one draw needn't show every extreme that they name: `factor_old`: symmetric in its last two dimensions. `stale_inverse`: symmetric in its last two dimensions.
All inputs are finite; a program needn't handle non-finite values.
Results may differ from a plain program's by a relative error of at most 0.039.
Values may be sent and summed in bfloat16 or wider, within the bound.
No kernel may reach another device: no remote copies, remote signals or barrier semaphores. Data moves between devices by JAX's collectives and lax.ppermute only.
A program may use at most 128 MiB of HBM per device.

v0:
```python
import jax
import jax.numpy as jnp
from jax import lax
from jax.sharding import PartitionSpec as P

BETA = 0.25
DAMPING = 1.0


def from_behind(block, axis, distance):
    devices = range(lax.axis_size(axis))
    route = [(i - distance, i) for i in devices if i - distance in devices]
    return lax.ppermute(block, axis, route)


def tanh_slope(preact):
    squashed = jnp.tanh(preact)
    return 1.0 - squashed * squashed


def per_device(inputs, cotangent, weight, factor_old, stale_inverse):
    section_id = lax.axis_index("section")
    sections = lax.axis_size("section")
    replicas = lax.axis_size("dp")
    weight_mat = weight[0]
    micros, tok_rows, feat_width = inputs.shape
    row_count = factor_old.shape[1]
    row_start = lax.axis_index("dp") * row_count
    ticks = micros + sections - 1
    contract_rows = (((0,), (0,)), ((), ()))

    def forward_work(current):
        preact = jnp.dot(current, weight_mat, preferred_element_type=jnp.float32)
        leaving = (current.astype(jnp.float32) + jnp.tanh(preact)).astype(jnp.bfloat16)
        return (leaving, preact)

    def forward_skip(current):
        return (current, jnp.zeros(current.shape, jnp.float32))

    def forward_tick(carried, tick_no):
        arriving, stored, preacts, gram_sum = carried
        micro_idx = tick_no - section_id
        is_valid = (micro_idx >= 0) & (micro_idx < micros)
        slot_idx = jnp.clip(micro_idx, 0, micros - 1)
        fresh_rows = lax.dynamic_index_in_dim(
            inputs, jnp.clip(tick_no, 0, micros - 1), 0, keepdims=False
        )
        current = jnp.where(section_id == 0, fresh_rows, arriving)
        leaving, preact = lax.cond(is_valid, forward_work, forward_skip, current)
        stored = jnp.where(
            is_valid, lax.dynamic_update_index_in_dim(stored, current, slot_idx, 0), stored
        )
        preacts = jnp.where(
            is_valid, lax.dynamic_update_index_in_dim(preacts, preact, slot_idx, 0), preacts
        )
        arriving = from_behind(leaving, "section", 1)
        return ((arriving, stored, preacts, gram_sum), None)

    gram_init = jnp.zeros((1,), jnp.float32)
    start_state = (
        jnp.zeros((tok_rows, feat_width), jnp.bfloat16),
        jnp.zeros_like(inputs),
        jnp.zeros(inputs.shape, jnp.float32),
        gram_init,
    )
    forward_state, unused = lax.scan(forward_tick, start_state, jnp.arange(ticks, dtype=jnp.int32))
    arriving_last, stored, preacts, gram_sum = forward_state

    def backward_tick(carried, tick_no):
        arriving, grads = carried
        micro_idx = tick_no - (sections - 1 - section_id)
        is_valid = (micro_idx >= 0) & (micro_idx < micros)
        slot_idx = jnp.clip(micro_idx, 0, micros - 1)
        fresh_rows = lax.dynamic_index_in_dim(
            cotangent, jnp.clip(tick_no, 0, micros - 1), 0, keepdims=False
        )
        current = jnp.where(section_id == sections - 1, fresh_rows, arriving)
        preact = lax.dynamic_index_in_dim(preacts, slot_idx, 0, keepdims=False)

        def backward_work(upstream):
            upstream_f = upstream.astype(jnp.float32)
            scaled = (upstream_f * tanh_slope(preact)).astype(jnp.bfloat16)
            back = lax.dot_general(
                scaled, weight_mat, (((1,), (1,)), ((), ())), preferred_element_type=jnp.float32
            )
            return (upstream_f + back).astype(jnp.bfloat16)

        def backward_skip(upstream):
            return upstream

        leaving = lax.cond(is_valid, backward_work, backward_skip, current)
        grads = jnp.where(
            is_valid, lax.dynamic_update_index_in_dim(grads, leaving, slot_idx, 0), grads
        )
        arriving = from_behind(leaving, "section", -1)
        return ((arriving, grads), None)

    back_state = (jnp.zeros((tok_rows, feat_width), jnp.bfloat16), jnp.zeros_like(cotangent))
    backward_state, unused_too = lax.scan(
        backward_tick, back_state, jnp.arange(ticks, dtype=jnp.int32)
    )
    arriving_first, grads = backward_state
    flat_rows = stored.reshape(-1, feat_width)
    gram_rows = lax.psum_scatter(
        lax.dot_general(
            flat_rows, flat_rows, contract_rows, preferred_element_type=jnp.float32
        ).astype(jnp.bfloat16),
        "dp",
        scatter_dimension=0,
        tiled=True,
    ).astype(jnp.float32)
    total_tokens = micros * tok_rows * replicas
    factor = BETA * factor_old[0] + (1.0 - BETA) / total_tokens * gram_rows
    column_ids = lax.broadcasted_iota(jnp.int32, (row_count, feat_width), 1)
    row_ids = lax.broadcasted_iota(jnp.int32, (row_count, feat_width), 0) + row_start
    damped = (factor + DAMPING * (column_ids == row_ids).astype(jnp.float32)).astype(jnp.bfloat16)
    stale_rows = stale_inverse[0]
    left_cols = damped
    product_rows = jnp.dot(
        left_cols,
        lax.all_gather(stale_rows, "dp", axis=0, tiled=True),
        preferred_element_type=jnp.float32,
    ).astype(jnp.bfloat16)
    left_cols = stale_rows
    correction = jnp.dot(
        left_cols,
        lax.all_gather(product_rows, "dp", axis=0, tiled=True),
        preferred_element_type=jnp.float32,
    )
    refined = (2.0 * stale_rows.astype(jnp.float32) - correction).astype(jnp.bfloat16)
    return (grads[None], factor[None], refined[None])


def solution(mesh):
    placed = (
        P(None, "dp", None),
        P(None, "dp", None),
        P("section", None, None),
        P("section", "dp", None),
        P("section", "dp", None),
    )
    return jax.shard_map(
        per_device,
        mesh=mesh,
        in_specs=placed,
        out_specs=(
            P("section", None, "dp", None),
            P("section", "dp", None),
            P("section", "dp", None),
        ),
        check_vma=False,
    )
```

profile of v0, /device:TPU:64, one launch (start us, length us, event | category | flops | bytes accessed | tf_op | source)
XLA Modules:
  0.0 789.6 jit_solution(3334653212232872092)
XLA Ops:
  9.3 243.5 %while.29 = (s32[]{:T(128)}, bf16[64,2048]{1,0:T(8,128)(2,1)S(1)}, bf16[4,64,2048]{2,1,0:T(8,128)(2,1)}, f32[4,64,2048]{2,1,0:T(8,128)S(1)}, s32[11]{0:T(128)S(1...) while((s32[]{:T(128)}, bf16[64,2048]{1,0:T(8,128)(2,1)S(1)}, ...), condition=%wide.region_3.4_spmd, body=%wide.region_0.3_spmd.sunk | while | flops 537657344 | bytes 13370165 | solution.py:66
  11.2 1.8 fusion.31
  13.1 5.0 conditional.4
  13.1 5.0 add_convert_fusion
  18.1 2.4 collective-permute-start
  20.6 16.0 %collective-permute-done = bf16[64,2048]{1,0:T(8,128)(2,1)S(1)} collective-permute-done((bf16[64,2048]{1,0:T(8,128)(2,1)S(1)}, bf16[64,2048]{1,0:T(8,128)(2,1)S(1)}, u32[]{:S(2)}, u32[]{:S(2)}) %collective-permute-start) | collective-permute-done | bytes 262176 | tf_op jit(solution)/shard_map/while/body/eval_jaxpr/ppermute | solution.py:13
  38.5 1.9 fusion.31
  40.3 5.1 conditional.4
  40.3 5.1 add_convert_fusion
  45.5 8.8 %collective-permute-start = (bf16[64,2048]{1,0:T(8,128)(2,1)S(1)}, bf16[64,2048]{1,0:T(8,128)(2,1)S(1)}, u32[]{:S(2)}, u32[]{:S(2)}) collective-permute-start(bf16[64,2048]{1,0:T(8,128)(2,1)S(1)} %get-tuple-element.377), channel_id=1, source_target_pairs={{0,32},{32,64},{64,96},{96,128},{128,160},{160,192},{192,224},{1,3... | collective-permute-start | bytes 786440 | tf_op jit(solution)/shard_map/while/body/eval_jaxpr/ppermute | solution.py:13
  54.4 13.9 %collective-permute-done = bf16[64,2048]{1,0:T(8,128)(2,1)S(1)} collective-permute-done((bf16[64,2048]{1,0:T(8,128)(2,1)S(1)}, bf16[64,2048]{1,0:T(8,128)(2,1)S(1)}, u32[]{:S(2)}, u32[]{:S(2)}) %collective-permute-start) | collective-permute-done | bytes 262176 | tf_op jit(solution)/shard_map/while/body/eval_jaxpr/ppermute | solution.py:13
  70.2 1.8 fusion.31
  72.0 5.1 conditional.4
  72.0 5.1 add_convert_fusion
  77.1 8.8 %collective-permute-start = (bf16[64,2048]{1,0:T(8,128)(2,1)S(1)}, bf16[64,2048]{1,0:T(8,128)(2,1)S(1)}, u32[]{:S(2)}, u32[]{:S(2)}) collective-permute-start(bf16[64,2048]{1,0:T(8,128)(2,1)S(1)} %get-tuple-element.377), channel_id=1, source_target_pairs={{0,32},{32,64},{64,96},{96,128},{128,160},{160,192},{192,224},{1,3... | collective-permute-start | bytes 786440 | tf_op jit(solution)/shard_map/while/body/eval_jaxpr/ppermute | solution.py:13
  86.0 9.3 %collective-permute-done = bf16[64,2048]{1,0:T(8,128)(2,1)S(1)} collective-permute-done((bf16[64,2048]{1,0:T(8,128)(2,1)S(1)}, bf16[64,2048]{1,0:T(8,128)(2,1)S(1)}, u32[]{:S(2)}, u32[]{:S(2)}) %collective-permute-start) | collective-permute-done | bytes 262176 | tf_op jit(solution)/shard_map/while/body/eval_jaxpr/ppermute | solution.py:13
  97.2 1.8 fusion.31
  99.1 5.1 conditional.4
  99.1 5.1 add_convert_fusion
  104.2 8.6 %collective-permute-start = (bf16[64,2048]{1,0:T(8,128)(2,1)S(1)}, bf16[64,2048]{1,0:T(8,128)(2,1)S(1)}, u32[]{:S(2)}, u32[]{:S(2)}) collective-permute-start(bf16[64,2048]{1,0:T(8,128)(2,1)S(1)} %get-tuple-element.377), channel_id=1, source_target_pairs={{0,32},{32,64},{64,96},{96,128},{128,160},{160,192},{192,224},{1,3... | collective-permute-start | bytes 786440 | tf_op jit(solution)/shard_map/while/body/eval_jaxpr/ppermute | solution.py:13
  112.8 3.8 collective-permute-done
  118.5 1.8 fusion.31
  120.4 13.3 %collective-permute-start = (bf16[64,2048]{1,0:T(8,128)(2,1)S(1)}, bf16[64,2048]{1,0:T(8,128)(2,1)S(1)}, u32[]{:S(2)}, u32[]{:S(2)}) collective-permute-start(bf16[64,2048]{1,0:T(8,128)(2,1)S(1)} %get-tuple-element.377), channel_id=1, source_target_pairs={{0,32},{32,64},{64,96},{96,128},{128,160},{160,192},{192,224},{1,3... | collective-permute-start | bytes 786440 | tf_op jit(solution)/shard_map/while/body/eval_jaxpr/ppermute | solution.py:13
  133.8 3.8 collective-permute-done
  139.5 1.8 fusion.31
  141.4 8.3 %collective-permute-start = (bf16[64,2048]{1,0:T(8,128)(2,1)S(1)}, bf16[64,2048]{1,0:T(8,128)(2,1)S(1)}, u32[]{:S(2)}, u32[]{:S(2)}) collective-permute-start(bf16[64,2048]{1,0:T(8,128)(2,1)S(1)} %get-tuple-element.377), channel_id=1, source_target_pairs={{0,32},{32,64},{64,96},{96,128},{128,160},{160,192},{192,224},{1,3... | collective-permute-start | bytes 786440 | tf_op jit(solution)/shard_map/while/body/eval_jaxpr/ppermute | solution.py:13
  149.8 3.8 collective-permute-done
  155.5 1.8 fusion.31
  157.4 16.2 %collective-permute-start = (bf16[64,2048]{1,0:T(8,128)(2,1)S(1)}, bf16[64,2048]{1,0:T(8,128)(2,1)S(1)}, u32[]{:S(2)}, u32[]{:S(2)}) collective-permute-start(bf16[64,2048]{1,0:T(8,128)(2,1)S(1)} %get-tuple-element.377), channel_id=1, source_target_pairs={{0,32},{32,64},{64,96},{96,128},{128,160},{160,192},{192,224},{1,3... | collective-permute-start | bytes 786440 | tf_op jit(solution)/shard_map/while/body/eval_jaxpr/ppermute | solution.py:13
  173.7 5.0 collective-permute-done
  180.6 1.8 fusion.31
  182.5 9.7 %collective-permute-start = (bf16[64,2048]{1,0:T(8,128)(2,1)S(1)}, bf16[64,2048]{1,0:T(8,128)(2,1)S(1)}, u32[]{:S(2)}, u32[]{:S(2)}) collective-permute-start(bf16[64,2048]{1,0:T(8,128)(2,1)S(1)} %get-tuple-element.377), channel_id=1, source_target_pairs={{0,32},{32,64},{64,96},{96,128},{128,160},{160,192},{192,224},{1,3... | collective-permute-start | bytes 786440 | tf_op jit(solution)/shard_map/while/body/eval_jaxpr/ppermute | solution.py:13
  192.3 5.9 collective-permute-done
  202.0 8.7 %collective-permute-start = (bf16[64,2048]{1,0:T(8,128)(2,1)S(1)}, bf16[64,2048]{1,0:T(8,128)(2,1)S(1)}, u32[]{:S(2)}, u32[]{:S(2)}) collective-permute-start(bf16[64,2048]{1,0:T(8,128)(2,1)S(1)} %get-tuple-element.377), channel_id=1, source_target_pairs={{0,32},{32,64},{64,96},{96,128},{128,160},{160,192},{192,224},{1,3... | collective-permute-start | bytes 786440 | tf_op jit(solution)/shard_map/while/body/eval_jaxpr/ppermute | solution.py:13
  210.9 4.9 collective-permute-done
  219.6 10.8 %collective-permute-start = (bf16[64,2048]{1,0:T(8,128)(2,1)S(1)}, bf16[64,2048]{1,0:T(8,128)(2,1)S(1)}, u32[]{:S(2)}, u32[]{:S(2)}) collective-permute-start(bf16[64,2048]{1,0:T(8,128)(2,1)S(1)} %get-tuple-element.377), channel_id=1, source_target_pairs={{0,32},{32,64},{64,96},{96,128},{128,160},{160,192},{192,224},{1,3... | collective-permute-start | bytes 786440 | tf_op jit(solution)/shard_map/while/body/eval_jaxpr/ppermute | solution.py:13
  230.6 6.2 collective-permute-done
  240.6 8.4 %collective-permute-start = (bf16[64,2048]{1,0:T(8,128)(2,1)S(1)}, bf16[64,2048]{1,0:T(8,128)(2,1)S(1)}, u32[]{:S(2)}, u32[]{:S(2)}) collective-permute-start(bf16[64,2048]{1,0:T(8,128)(2,1)S(1)} %get-tuple-element.377), channel_id=1, source_target_pairs={{0,32},{32,64},{64,96},{96,128},{128,160},{160,192},{192,224},{1,3... | collective-permute-start | bytes 786440 | tf_op jit(solution)/shard_map/while/body/eval_jaxpr/ppermute | solution.py:13
  249.1 3.8 collective-permute-done
  252.8 7.2 bitcast_convert_fusion
  260.2 152.8 %reduce-scatter.2.cloned.1.call-done = bf16[64,2048]{1,0:T(8,128)(2,1)} async-done(((bf16[2048,2048]{1,0:T(8,128)(2,1)}), bf16[64,2048]{1,0:T(8,128)(2,1)}) %reduce-scatter.2.cloned.1.call-update) | async-done | bytes 262160 | tf_op jit(solution)/shard_map/reduce_scatter | solution.py:104
  413.1 5.8 fusion.12
  419.8 94.2 %all-gather.4.cloned.1.call-done = bf16[2048,2048]{1,0:T(8,128)(2,1)} async-done(((bf16[64,2048]{1,0:T(8,128)(2,1)}), bf16[2048,2048]{1,0:T(8,128)(2,1)}) %all-gather.4.cloned.1.call-update) | async-done | bytes 8388624 | tf_op jit(solution)/shard_map/all_gather | solution.py:127
  514.0 5.7 fusion.15
  520.8 262.2 %while.30 = (s32[]{:T(128)}, bf16[64,2048]{1,0:T(8,128)(2,1)S(1)}, bf16[4,64,2048]{2,1,0:T(8,128)(2,1)}, s32[11]{0:T(128)S(1)}, s32[]{:T(128)}, /*index=5*/pred[...) while((s32[]{:T(128)}, bf16[64,2048]{1,0:T(8,128)(2,1)S(1)}, ...), condition=%wide.region_7.8_spmd, body=%wide.region_4.7_spmd.sunk | while | flops 538181632 | bytes 12845881 | solution.py:99
  526.9 16.8 %collective-permute-done.1 = bf16[64,2048]{1,0:T(8,128)(2,1)S(1)} collective-permute-done((bf16[64,2048]{1,0:T(8,128)(2,1)S(1)}, bf16[64,2048]{1,0:T(8,128)(2,1)S(1)}, u32[]{:S(2)}, u32[]{:S(2)}) %collective-permute-start.1) | collective-permute-done | bytes 262176 | tf_op jit(solution)/shard_map/while/body/eval_jaxpr/ppermute | solution.py:13
  549.8 13.2 %collective-permute-done.1 = bf16[64,2048]{1,0:T(8,128)(2,1)S(1)} collective-permute-done((bf16[64,2048]{1,0:T(8,128)(2,1)S(1)}, bf16[64,2048]{1,0:T(8,128)(2,1)S(1)}, u32[]{:S(2)}, u32[]{:S(2)}) %collective-permute-start.1) | collective-permute-done | bytes 262176 | tf_op jit(solution)/shard_map/while/body/eval_jaxpr/ppermute | solution.py:13
  569.2 17.4 %collective-permute-done.1 = bf16[64,2048]{1,0:T(8,128)(2,1)S(1)} collective-permute-done((bf16[64,2048]{1,0:T(8,128)(2,1)S(1)}, bf16[64,2048]{1,0:T(8,128)(2,1)S(1)}, u32[]{:S(2)}, u32[]{:S(2)}) %collective-permute-start.1) | collective-permute-done | bytes 262176 | tf_op jit(solution)/shard_map/while/body/eval_jaxpr/ppermute | solution.py:13
  592.6 13.5 %collective-permute-done.1 = bf16[64,2048]{1,0:T(8,128)(2,1)S(1)} collective-permute-done((bf16[64,2048]{1,0:T(8,128)(2,1)S(1)}, bf16[64,2048]{1,0:T(8,128)(2,1)S(1)}, u32[]{:S(2)}, u32[]{:S(2)}) %collective-permute-start.1) | collective-permute-done | bytes 262176 | tf_op jit(solution)/shard_map/while/body/eval_jaxpr/ppermute | solution.py:13
  612.2 14.8 %collective-permute-done.1 = bf16[64,2048]{1,0:T(8,128)(2,1)S(1)} collective-permute-done((bf16[64,2048]{1,0:T(8,128)(2,1)S(1)}, bf16[64,2048]{1,0:T(8,128)(2,1)S(1)}, u32[]{:S(2)}, u32[]{:S(2)}) %collective-permute-start.1) | collective-permute-done | bytes 262176 | tf_op jit(solution)/shard_map/while/body/eval_jaxpr/ppermute | solution.py:13
  633.1 11.1 %collective-permute-done.1 = bf16[64,2048]{1,0:T(8,128)(2,1)S(1)} collective-permute-done((bf16[64,2048]{1,0:T(8,128)(2,1)S(1)}, bf16[64,2048]{1,0:T(8,128)(2,1)S(1)}, u32[]{:S(2)}, u32[]{:S(2)}) %collective-permute-start.1) | collective-permute-done | bytes 262176 | tf_op jit(solution)/shard_map/while/body/eval_jaxpr/ppermute | solution.py:13
  650.3 24.8 %collective-permute-done.1 = bf16[64,2048]{1,0:T(8,128)(2,1)S(1)} collective-permute-done((bf16[64,2048]{1,0:T(8,128)(2,1)S(1)}, bf16[64,2048]{1,0:T(8,128)(2,1)S(1)}, u32[]{:S(2)}, u32[]{:S(2)}) %collective-permute-start.1) | collective-permute-done | bytes 262176 | tf_op jit(solution)/shard_map/while/body/eval_jaxpr/ppermute | solution.py:13
  678.2 6.1 conditional.5
  678.2 6.0 fusion.1
  687.3 22.3 %collective-permute-done.1 = bf16[64,2048]{1,0:T(8,128)(2,1)S(1)} collective-permute-done((bf16[64,2048]{1,0:T(8,128)(2,1)S(1)}, bf16[64,2048]{1,0:T(8,128)(2,1)S(1)}, u32[]{:S(2)}, u32[]{:S(2)}) %collective-permute-start.1) | collective-permute-done | bytes 262176 | tf_op jit(solution)/shard_map/while/body/eval_jaxpr/ppermute | solution.py:13
  712.6 6.1 conditional.5
  712.7 6.0 fusion.1
  721.7 17.0 %collective-permute-done.1 = bf16[64,2048]{1,0:T(8,128)(2,1)S(1)} collective-permute-done((bf16[64,2048]{1,0:T(8,128)(2,1)S(1)}, bf16[64,2048]{1,0:T(8,128)(2,1)S(1)}, u32[]{:S(2)}, u32[]{:S(2)}) %collective-permute-start.1) | collective-permute-done | bytes 262176 | tf_op jit(solution)/shard_map/while/body/eval_jaxpr/ppermute | solution.py:13
  741.8 6.1 conditional.5
  741.9 6.0 fusion.1
  750.9 10.8 %collective-permute-done.1 = bf16[64,2048]{1,0:T(8,128)(2,1)S(1)} collective-permute-done((bf16[64,2048]{1,0:T(8,128)(2,1)S(1)}, bf16[64,2048]{1,0:T(8,128)(2,1)S(1)}, u32[]{:S(2)}, u32[]{:S(2)}) %collective-permute-start.1) | collective-permute-done | bytes 262176 | tf_op jit(solution)/shard_map/while/body/eval_jaxpr/ppermute | solution.py:13
  764.7 6.1 conditional.5
  764.8 6.0 fusion.1
  773.8 9.2 %collective-permute-done.1 = bf16[64,2048]{1,0:T(8,128)(2,1)S(1)} collective-permute-done((bf16[64,2048]{1,0:T(8,128)(2,1)S(1)}, bf16[64,2048]{1,0:T(8,128)(2,1)S(1)}, u32[]{:S(2)}, u32[]{:S(2)}) %collective-permute-start.1) | collective-permute-done | bytes 262176 | tf_op jit(solution)/shard_map/while/body/eval_jaxpr/ppermute | solution.py:13
  (123 shorter events, 70.0 us)
Async XLA Ops:
  7.2 253.1 %all-gather.6.cloned.1.call-start = ((), (), s32[]{:S(2)}) async-start(), calls=%async_computation.3 | async-start | bytes 8650752 | tf_op jit(solution)/shard_map/all_gather | solution.py:121
  7.9 405.2 %reduce-scatter.2.cloned.1.call-start = ((), (), s32[]{:S(2)}) async-start(), calls=%async_computation.1 | async-start | bytes 8650752 | tf_op jit(solution)/shard_map/reduce_scatter | solution.py:104
  18.1 18.5 %collective-permute-start = (bf16[64,2048]{1,0:T(8,128)(2,1)S(1)}, bf16[64,2048]{1,0:T(8,128)(2,1)S(1)}, u32[]{:S(2)}, u32[]{:S(2)}) collective-permute-start(bf16[64,2048]{1,0:T(8,128)(2,1)S(1)} %get-tuple-element.377), channel_id=1, source_target_pairs={{0,32},{32,64},{64,96},{96,128},{128,160},{160,192},{192,224},{1,3... | collective-permute-start | bytes 786440 | tf_op jit(solution)/shard_map/while/body/eval_jaxpr/ppermute | solution.py:13
  45.5 22.8 %collective-permute-start = (bf16[64,2048]{1,0:T(8,128)(2,1)S(1)}, bf16[64,2048]{1,0:T(8,128)(2,1)S(1)}, u32[]{:S(2)}, u32[]{:S(2)}) collective-permute-start(bf16[64,2048]{1,0:T(8,128)(2,1)S(1)} %get-tuple-element.377), channel_id=1, source_target_pairs={{0,32},{32,64},{64,96},{96,128},{128,160},{160,192},{192,224},{1,3... | collective-permute-start | bytes 786440 | tf_op jit(solution)/shard_map/while/body/eval_jaxpr/ppermute | solution.py:13
  77.1 18.2 %collective-permute-start = (bf16[64,2048]{1,0:T(8,128)(2,1)S(1)}, bf16[64,2048]{1,0:T(8,128)(2,1)S(1)}, u32[]{:S(2)}, u32[]{:S(2)}) collective-permute-start(bf16[64,2048]{1,0:T(8,128)(2,1)S(1)} %get-tuple-element.377), channel_id=1, source_target_pairs={{0,32},{32,64},{64,96},{96,128},{128,160},{160,192},{192,224},{1,3... | collective-permute-start | bytes 786440 | tf_op jit(solution)/shard_map/while/body/eval_jaxpr/ppermute | solution.py:13
  104.2 12.4 %collective-permute-start = (bf16[64,2048]{1,0:T(8,128)(2,1)S(1)}, bf16[64,2048]{1,0:T(8,128)(2,1)S(1)}, u32[]{:S(2)}, u32[]{:S(2)}) collective-permute-start(bf16[64,2048]{1,0:T(8,128)(2,1)S(1)} %get-tuple-element.377), channel_id=1, source_target_pairs={{0,32},{32,64},{64,96},{96,128},{128,160},{160,192},{192,224},{1,3... | collective-permute-start | bytes 786440 | tf_op jit(solution)/shard_map/while/body/eval_jaxpr/ppermute | solution.py:13
  120.4 17.2 %collective-permute-start = (bf16[64,2048]{1,0:T(8,128)(2,1)S(1)}, bf16[64,2048]{1,0:T(8,128)(2,1)S(1)}, u32[]{:S(2)}, u32[]{:S(2)}) collective-permute-start(bf16[64,2048]{1,0:T(8,128)(2,1)S(1)} %get-tuple-element.377), channel_id=1, source_target_pairs={{0,32},{32,64},{64,96},{96,128},{128,160},{160,192},{192,224},{1,3... | collective-permute-start | bytes 786440 | tf_op jit(solution)/shard_map/while/body/eval_jaxpr/ppermute | solution.py:13
  141.4 12.2 %collective-permute-start = (bf16[64,2048]{1,0:T(8,128)(2,1)S(1)}, bf16[64,2048]{1,0:T(8,128)(2,1)S(1)}, u32[]{:S(2)}, u32[]{:S(2)}) collective-permute-start(bf16[64,2048]{1,0:T(8,128)(2,1)S(1)} %get-tuple-element.377), channel_id=1, source_target_pairs={{0,32},{32,64},{64,96},{96,128},{128,160},{160,192},{192,224},{1,3... | collective-permute-start | bytes 786440 | tf_op jit(solution)/shard_map/while/body/eval_jaxpr/ppermute | solution.py:13
  157.4 21.3 %collective-permute-start = (bf16[64,2048]{1,0:T(8,128)(2,1)S(1)}, bf16[64,2048]{1,0:T(8,128)(2,1)S(1)}, u32[]{:S(2)}, u32[]{:S(2)}) collective-permute-start(bf16[64,2048]{1,0:T(8,128)(2,1)S(1)} %get-tuple-element.377), channel_id=1, source_target_pairs={{0,32},{32,64},{64,96},{96,128},{128,160},{160,192},{192,224},{1,3... | collective-permute-start | bytes 786440 | tf_op jit(solution)/shard_map/while/body/eval_jaxpr/ppermute | solution.py:13
  182.5 15.7 %collective-permute-start = (bf16[64,2048]{1,0:T(8,128)(2,1)S(1)}, bf16[64,2048]{1,0:T(8,128)(2,1)S(1)}, u32[]{:S(2)}, u32[]{:S(2)}) collective-permute-start(bf16[64,2048]{1,0:T(8,128)(2,1)S(1)} %get-tuple-element.377), channel_id=1, source_target_pairs={{0,32},{32,64},{64,96},{96,128},{128,160},{160,192},{192,224},{1,3... | collective-permute-start | bytes 786440 | tf_op jit(solution)/shard_map/while/body/eval_jaxpr/ppermute | solution.py:13
  202.0 13.8 %collective-permute-start = (bf16[64,2048]{1,0:T(8,128)(2,1)S(1)}, bf16[64,2048]{1,0:T(8,128)(2,1)S(1)}, u32[]{:S(2)}, u32[]{:S(2)}) collective-permute-start(bf16[64,2048]{1,0:T(8,128)(2,1)S(1)} %get-tuple-element.377), channel_id=1, source_target_pairs={{0,32},{32,64},{64,96},{96,128},{128,160},{160,192},{192,224},{1,3... | collective-permute-start | bytes 786440 | tf_op jit(solution)/shard_map/while/body/eval_jaxpr/ppermute | solution.py:13
  219.6 17.1 %collective-permute-start = (bf16[64,2048]{1,0:T(8,128)(2,1)S(1)}, bf16[64,2048]{1,0:T(8,128)(2,1)S(1)}, u32[]{:S(2)}, u32[]{:S(2)}) collective-permute-start(bf16[64,2048]{1,0:T(8,128)(2,1)S(1)} %get-tuple-element.377), channel_id=1, source_target_pairs={{0,32},{32,64},{64,96},{96,128},{128,160},{160,192},{192,224},{1,3... | collective-permute-start | bytes 786440 | tf_op jit(solution)/shard_map/while/body/eval_jaxpr/ppermute | solution.py:13
  240.6 12.3 %collective-permute-start = (bf16[64,2048]{1,0:T(8,128)(2,1)S(1)}, bf16[64,2048]{1,0:T(8,128)(2,1)S(1)}, u32[]{:S(2)}, u32[]{:S(2)}) collective-permute-start(bf16[64,2048]{1,0:T(8,128)(2,1)S(1)} %get-tuple-element.377), channel_id=1, source_target_pairs={{0,32},{32,64},{64,96},{96,128},{128,160},{160,192},{192,224},{1,3... | collective-permute-start | bytes 786440 | tf_op jit(solution)/shard_map/while/body/eval_jaxpr/ppermute | solution.py:13
  260.1 153.0 %copy-start = (f32[1,64,2048]{2,1,0:T(8,128)S(1)}, f32[1,64,2048]{2,1,0:T(8,128)}, u32[]{:S(2)}) copy-start(f32[1,64,2048]{2,1,0:T(8,128)} %param.16) | copy-start | bytes 1572868
  260.1 253.9 %all-gather.4.cloned.1.call-start = ((), (), s32[]{:S(2)}) async-start(), calls=%async_computation.2 | async-start | bytes 8650752 | tf_op jit(solution)/shard_map/all_gather | solution.py:127
  260.2 253.9 %copy-start.2 = (bf16[1,64,2048]{2,1,0:T(8,128)(2,1)S(1)}, bf16[1,64,2048]{2,1,0:T(8,128)(2,1)}, u32[]{:S(2)}) copy-start(bf16[1,64,2048]{2,1,0:T(8,128)(2,1)} %param.17) | copy-start | bytes 786436
  413.1 5.9 copy-start.1
  523.9 19.9 %collective-permute-start.1 = (bf16[64,2048]{1,0:T(8,128)(2,1)S(1)}, bf16[64,2048]{1,0:T(8,128)(2,1)S(1)}, u32[]{:S(2)}, u32[]{:S(2)}) collective-permute-start(bf16[64,2048]{1,0:T(8,128)(2,1)S(1)} %get-tuple-element.471), channel_id=1, source_target_pairs={{32,0},{64,32},{96,64},{128,96},{160,128},{192,160},{224,192},{33,... | collective-permute-start | bytes 786440 | tf_op jit(solution)/shard_map/while/body/eval_jaxpr/ppermute | solution.py:13
  546.8 16.2 %collective-permute-start.1 = (bf16[64,2048]{1,0:T(8,128)(2,1)S(1)}, bf16[64,2048]{1,0:T(8,128)(2,1)S(1)}, u32[]{:S(2)}, u32[]{:S(2)}) collective-permute-start(bf16[64,2048]{1,0:T(8,128)(2,1)S(1)} %get-tuple-element.471), channel_id=1, source_target_pairs={{32,0},{64,32},{96,64},{128,96},{160,128},{192,160},{224,192},{33,... | collective-permute-start | bytes 786440 | tf_op jit(solution)/shard_map/while/body/eval_jaxpr/ppermute | solution.py:13
  566.1 20.4 %collective-permute-start.1 = (bf16[64,2048]{1,0:T(8,128)(2,1)S(1)}, bf16[64,2048]{1,0:T(8,128)(2,1)S(1)}, u32[]{:S(2)}, u32[]{:S(2)}) collective-permute-start(bf16[64,2048]{1,0:T(8,128)(2,1)S(1)} %get-tuple-element.471), channel_id=1, source_target_pairs={{32,0},{64,32},{96,64},{128,96},{160,128},{192,160},{224,192},{33,... | collective-permute-start | bytes 786440 | tf_op jit(solution)/shard_map/while/body/eval_jaxpr/ppermute | solution.py:13
  589.6 16.6 %collective-permute-start.1 = (bf16[64,2048]{1,0:T(8,128)(2,1)S(1)}, bf16[64,2048]{1,0:T(8,128)(2,1)S(1)}, u32[]{:S(2)}, u32[]{:S(2)}) collective-permute-start(bf16[64,2048]{1,0:T(8,128)(2,1)S(1)} %get-tuple-element.471), channel_id=1, source_target_pairs={{32,0},{64,32},{96,64},{128,96},{160,128},{192,160},{224,192},{33,... | collective-permute-start | bytes 786440 | tf_op jit(solution)/shard_map/while/body/eval_jaxpr/ppermute | solution.py:13
  609.2 17.8 %collective-permute-start.1 = (bf16[64,2048]{1,0:T(8,128)(2,1)S(1)}, bf16[64,2048]{1,0:T(8,128)(2,1)S(1)}, u32[]{:S(2)}, u32[]{:S(2)}) collective-permute-start(bf16[64,2048]{1,0:T(8,128)(2,1)S(1)} %get-tuple-element.471), channel_id=1, source_target_pairs={{32,0},{64,32},{96,64},{128,96},{160,128},{192,160},{224,192},{33,... | collective-permute-start | bytes 786440 | tf_op jit(solution)/shard_map/while/body/eval_jaxpr/ppermute | solution.py:13
  630.1 14.2 %collective-permute-start.1 = (bf16[64,2048]{1,0:T(8,128)(2,1)S(1)}, bf16[64,2048]{1,0:T(8,128)(2,1)S(1)}, u32[]{:S(2)}, u32[]{:S(2)}) collective-permute-start(bf16[64,2048]{1,0:T(8,128)(2,1)S(1)} %get-tuple-element.471), channel_id=1, source_target_pairs={{32,0},{64,32},{96,64},{128,96},{160,128},{192,160},{224,192},{33,... | collective-permute-start | bytes 786440 | tf_op jit(solution)/shard_map/while/body/eval_jaxpr/ppermute | solution.py:13
  647.3 27.8 %collective-permute-start.1 = (bf16[64,2048]{1,0:T(8,128)(2,1)S(1)}, bf16[64,2048]{1,0:T(8,128)(2,1)S(1)}, u32[]{:S(2)}, u32[]{:S(2)}) collective-permute-start(bf16[64,2048]{1,0:T(8,128)(2,1)S(1)} %get-tuple-element.471), channel_id=1, source_target_pairs={{32,0},{64,32},{96,64},{128,96},{160,128},{192,160},{224,192},{33,... | collective-permute-start | bytes 786440 | tf_op jit(solution)/shard_map/while/body/eval_jaxpr/ppermute | solution.py:13
  684.3 25.3 %collective-permute-start.1 = (bf16[64,2048]{1,0:T(8,128)(2,1)S(1)}, bf16[64,2048]{1,0:T(8,128)(2,1)S(1)}, u32[]{:S(2)}, u32[]{:S(2)}) collective-permute-start(bf16[64,2048]{1,0:T(8,128)(2,1)S(1)} %get-tuple-element.471), channel_id=1, source_target_pairs={{32,0},{64,32},{96,64},{128,96},{160,128},{192,160},{224,192},{33,... | collective-permute-start | bytes 786440 | tf_op jit(solution)/shard_map/while/body/eval_jaxpr/ppermute | solution.py:13
  718.7 20.1 %collective-permute-start.1 = (bf16[64,2048]{1,0:T(8,128)(2,1)S(1)}, bf16[64,2048]{1,0:T(8,128)(2,1)S(1)}, u32[]{:S(2)}, u32[]{:S(2)}) collective-permute-start(bf16[64,2048]{1,0:T(8,128)(2,1)S(1)} %get-tuple-element.471), channel_id=1, source_target_pairs={{32,0},{64,32},{96,64},{128,96},{160,128},{192,160},{224,192},{33,... | collective-permute-start | bytes 786440 | tf_op jit(solution)/shard_map/while/body/eval_jaxpr/ppermute | solution.py:13
  747.9 13.8 %collective-permute-start.1 = (bf16[64,2048]{1,0:T(8,128)(2,1)S(1)}, bf16[64,2048]{1,0:T(8,128)(2,1)S(1)}, u32[]{:S(2)}, u32[]{:S(2)}) collective-permute-start(bf16[64,2048]{1,0:T(8,128)(2,1)S(1)} %get-tuple-element.471), channel_id=1, source_target_pairs={{32,0},{64,32},{96,64},{128,96},{160,128},{192,160},{224,192},{33,... | collective-permute-start | bytes 786440 | tf_op jit(solution)/shard_map/while/body/eval_jaxpr/ppermute | solution.py:13
  770.8 12.2 %collective-permute-start.1 = (bf16[64,2048]{1,0:T(8,128)(2,1)S(1)}, bf16[64,2048]{1,0:T(8,128)(2,1)S(1)}, u32[]{:S(2)}, u32[]{:S(2)}) collective-permute-start(bf16[64,2048]{1,0:T(8,128)(2,1)S(1)} %get-tuple-element.471), channel_id=1, source_target_pairs={{32,0},{64,32},{96,64},{128,96},{160,128},{192,160},{224,192},{33,... | collective-permute-start | bytes 786440 | tf_op jit(solution)/shard_map/while/body/eval_jaxpr/ppermute | solution.py:13
Sparse Core Ops, SparseCore 0:
  9.9 96.1 all-gather.5
  260.2 152.7 reduce-scatter.1
  419.0 94.9 all-gather.3
where the time goes:
time: 794 us; the launch traced here: 790 us
  waiting for transfers between devices  495 us (62%)
  starting transfers between devices  118 us (15%)
  matrix products  63.2 us (8%)
  other arithmetic  51.9 us (7%)
  loops' own time  30 us (4%)
  local copies, waits for them, and re-layouts  17.3 us (2%)
  between operations  13.8 us (2%)
    ppermute x22, waiting for transfers between devices, from_behind(): return lax.ppermute(block, axis, route)  247 us
    reduce_scatter x1, waiting for transfers between devices, per_device(): lax.psum_scatter(lax.dot_general(flat_rows, flat_rows, contract_rows, pre...  153 us
    ppermute x22, starting transfers between devices, from_behind(): return lax.ppermute(block, axis, route)  118 us
    all_gather x1, waiting for transfers between devices, per_device(): lax.all_gather(product_rows, 'dp', axis=0, tiled=True)  94.2 us
    dot_general x4, matrix products, backward_work(): lax.dot_general(scaled, weight_mat, (((1,), (1,)), ((), ())), preferred_e...  24.2 us
    select_n x11, other arithmetic, forward_tick(): jnp.where(is_valid, lax.dynamic_update_index_in_dim(stored, current, slot...  20.3 us
    dot_general x4, matrix products, forward_work(): preact = jnp.dot(current, weight_mat, preferred_element_type=jnp.float32)  20.3 us
    select_n x11, other arithmetic, backward_tick(): jnp.where(is_valid, lax.dynamic_update_index_in_dim(grads, leaving, slot_...  18.9 us
  transfers between devices with their start and end apart: 25, of which 24 were waited for; matrix products, arithmetic and copies ran while one was open for 10% of the time, Pallas kernels for 0%

commit v1 on v0

v1 whole, which is shorter than its diff:
```python
import functools

import jax
import jax.numpy as jnp
from jax import lax
from jax.experimental import pallas as pl
from jax.experimental.pallas import tpu as pltpu
from jax.sharding import PartitionSpec as P

BETA = 0.25
DAMPING = 1.0

SECTIONS = 8
REPLICAS = 32
MICROS = 4
ROWS = 64
W = 2048
BLK = 256
NBLK = W // BLK
KEEP = NBLK // 2 + 1
KW = KEEP * BLK
LAST = SECTIONS - 1
TICKS = MICROS + SECTIONS - 1
SCALE = (1.0 - BETA) / (MICROS * ROWS * REPLICAS)

bf16 = jnp.bfloat16
f32 = jnp.float32

VM = pl.BlockSpec(memory_space=pltpu.VMEM)
ANY = pl.BlockSpec(memory_space=pl.ANY)

GROUP_XC = [[z * 8 + k for k in range(8)] for z in range(4)]
GROUP_Z = [[z * 8 + k for z in range(4)] for k in range(8)]


def call(kernel, out_shape, in_specs, out_specs, scratch, name, mib, flops=0, moved=0):
    return pl.pallas_call(
        kernel,
        out_shape=out_shape,
        in_specs=in_specs,
        out_specs=out_specs,
        scratch_shapes=scratch,
        compiler_params=pltpu.CompilerParams(vmem_limit_bytes=mib << 20),
        cost_estimate=pl.CostEstimate(flops=flops, bytes_accessed=moved, transcendentals=0),
        name=name,
    )


def rows_of(kind=bf16, rows=ROWS, cols=W):
    return jax.ShapeDtypeStruct((rows, cols), kind)


LAYER_COST = dict(flops=2 * ROWS * W * W, moved=W * W * 2)


def pick(index, choices, dst, sem):
    for number, src in enumerate(choices):

        @pl.when(index == number)
        def _():
            pltpu.make_async_copy(src, dst, sem).start()


def forward_layer(x_ref, w_ref, h_ref, slope_ref):
    for j in range(NBLK):
        cols = slice(j * BLK, (j + 1) * BLK)
        squashed = jnp.tanh(jnp.dot(x_ref[...], w_ref[:, cols], preferred_element_type=f32))
        h_ref[:, cols] = (x_ref[:, cols].astype(f32) + squashed).astype(bf16)
        slope_ref[:, cols] = (1.0 - squashed * squashed).astype(bf16)


def forward_tick(tick, inputs, arriving, weight):
    def kernel(inputs_ref, arriving_ref, w_ref, h_ref, slope_ref, x_scr, sem):
        section = lax.axis_index("section")
        micro = tick - section

        @pl.when((micro >= 0) & (micro < MICROS))
        def _():
            if tick < MICROS:

                @pl.when(section == 0)
                def _():
                    copy = pltpu.make_async_copy(inputs_ref.at[tick], x_scr, sem)
                    copy.start()
                    copy.wait()

            if tick > 0:

                @pl.when(section != 0)
                def _():
                    x_scr[...] = arriving_ref[...]

            forward_layer(x_scr, w_ref, h_ref, slope_ref)

    return call(
        kernel,
        [rows_of(), rows_of()],
        [ANY, VM, VM],
        [VM, VM],
        [pltpu.VMEM((ROWS, W), bf16), pltpu.SemaphoreType.DMA],
        "forward_tick",
        24,
        **LAYER_COST,
    )(inputs, arriving, weight)


def backward_tick(tick, cotangent, arriving, slopes, weight):
    def kernel(cot_ref, arriving_ref, w_ref, *rest):
        slope_refs = rest[: len(slopes)]
        g_ref, u_scr, slope_scr, scaled, sem, sem_slope = rest[len(slopes) :]
        section = lax.axis_index("section")
        micro = tick - (LAST - section)

        @pl.when((micro >= 0) & (micro < MICROS))
        def _():
            pick(section + micro, slope_refs, slope_scr, sem_slope)
            if tick < MICROS:

                @pl.when(section == LAST)
                def _():
                    copy = pltpu.make_async_copy(cot_ref.at[tick], u_scr, sem)
                    copy.start()
                    copy.wait()

            if tick > 0:

                @pl.when(section != LAST)
                def _():
                    u_scr[...] = arriving_ref[...]

            pltpu.make_async_copy(slope_refs[0], slope_scr, sem_slope).wait()
            scaled[...] = (u_scr[...].astype(f32) * slope_scr[...].astype(f32)).astype(bf16)
            for j in range(NBLK):
                cols = slice(j * BLK, (j + 1) * BLK)
                back = lax.dot_general(
                    scaled[...], w_ref[cols, :], (((1,), (1,)), ((), ())), preferred_element_type=f32
                )
                g_ref[:, cols] = (u_scr[:, cols].astype(f32) + back).astype(bf16)

    return call(
        kernel,
        rows_of(),
        [ANY, VM, VM] + [ANY] * len(slopes),
        VM,
        [pltpu.VMEM((ROWS, W), bf16)] * 3 + [pltpu.SemaphoreType.DMA] * 2,
        "backward_tick",
        24,
        **LAYER_COST,
    )(cotangent, arriving, weight, *slopes)


def gram(inputs, arrivals):
    def kernel(inputs_ref, *rest):
        arrival_refs = rest[: len(arrivals)]
        out_ref, hid, obuf, sems, osems = rest[len(arrivals) :]
        section = lax.axis_index("section")

        def slot(m):
            return hid.at[pl.ds(m * ROWS, ROWS), pl.ds(0, W)]

        for m in range(MICROS):

            @pl.when(section == 0)
            def _():
                pltpu.make_async_copy(inputs_ref.at[m], slot(m), sems.at[m]).start()

            pick(section + m - 1 + 100 * (section == 0).astype(jnp.int32), arrival_refs, slot(m), sems.at[m])
        for m in range(MICROS):
            pltpu.make_async_copy(inputs_ref.at[m], slot(m), sems.at[m]).wait()
        hid[:, W:] = hid[:, : KW - BLK]
        writes = []
        for i in range(NBLK):
            left = hid[:, i * BLK : (i + 1) * BLK]
            part = lax.dot_general(
                left, hid[:, i * BLK : i * BLK + KW], (((0,), (0,)), ((), ())), preferred_element_type=f32
            ).astype(bf16)
            for k in range(BLK // ROWS):
                device = i * (BLK // ROWS) + k
                at = (device % 8) * 4 + device // 8
                obuf[at * ROWS : (at + 1) * ROWS, :] = part[k * ROWS : (k + 1) * ROWS]
                span = pl.ds(at * ROWS, ROWS)
                copy = pltpu.make_async_copy(obuf.at[span], out_ref.at[span], osems.at[at])
                copy.start()
                writes.append(copy)
        for copy in writes:
            copy.wait()

    return call(
        kernel,
        rows_of(rows=W, cols=KW),
        [ANY] * (1 + len(arrivals)),
        ANY,
        [
            pltpu.VMEM((MICROS * ROWS, W + KW - BLK), bf16),
            pltpu.VMEM((W, KW), bf16),
            pltpu.SemaphoreType.DMA((MICROS,)),
            pltpu.SemaphoreType.DMA((REPLICAS,)),
        ],
        "gram",
        32,
        flops=2 * MICROS * ROWS * W * KW,
        moved=W * KW * 2,
    )(inputs, *arrivals)


def own_block():
    replica = lax.axis_index("dp")
    per_block = BLK // ROWS
    return replica // per_block, lax.rem(replica, per_block)


def block_cols(number):
    return pl.ds(pl.multiple_of(number * BLK, BLK), BLK)


def kept_columns(stale_rows):
    def kernel(s_ref, out_ref):
        block, part = own_block()
        for k in range(KEEP):
            out_ref[:, k * BLK : (k + 1) * BLK] = s_ref[:, block_cols(lax.rem(block + k, NBLK))]

    return call(kernel, rows_of(cols=KW), [VM], VM, [], "kept_columns", 8)(stale_rows)


def damped_rows(gram_rows, factor_old):
    def kernel(g_ref, f_ref, out_ref):
        block, part = own_block()
        for k in range(KEEP):
            cols = slice(k * BLK, (k + 1) * BLK)
            old = f_ref[:, block_cols(lax.rem(block + k, NBLK))]
            value = BETA * old + SCALE * g_ref[:, cols].astype(f32)
            if k == 0:
                column = lax.broadcasted_iota(jnp.int32, (ROWS, BLK), 1)
                row = lax.broadcasted_iota(jnp.int32, (ROWS, BLK), 0) + part * ROWS
                value = value + DAMPING * (column == row).astype(f32)
            out_ref[:, cols] = value.astype(bf16)

    return call(kernel, rows_of(cols=KW), [VM, VM], VM, [], "damped_rows", 8)(gram_rows, factor_old)


def times_symmetric(left_ref, mat_ref, j):
    total = None
    for i in range(NBLK):
        left = left_ref[:, i * BLK : (i + 1) * BLK]
        k = (j - i) % NBLK
        if k < KEEP:
            block = mat_ref[i * BLK : (i + 1) * BLK, k * BLK : (k + 1) * BLK]
            part = jnp.dot(left, block, preferred_element_type=f32)
        else:
            k = (i - j) % NBLK
            block = mat_ref[j * BLK : (j + 1) * BLK, k * BLK : (k + 1) * BLK]
            part = lax.dot_general(left, block, (((1,), (1,)), ((), ())), preferred_element_type=f32)
        total = part if total is None else total + part
    return total


def refresh(damped_all, stale_all, stale_rows, gram_rows, factor_old):
    def kernel(d_ref, sa_ref, s_ref, g_ref, f_ref, factor_ref, inv_ref, mid, turn):
        block, part = own_block()
        for j in range(NBLK):
            mid[:, j * BLK : (j + 1) * BLK] = times_symmetric(s_ref, d_ref, j).astype(bf16)
        for j in range(NBLK):
            cols = slice(j * BLK, (j + 1) * BLK)
            inv_ref[:, cols] = (2.0 * s_ref[:, cols].astype(f32) - times_symmetric(mid, sa_ref, j)).astype(bf16)
        for k in range(KEEP):
            cols = block_cols(lax.rem(block + k, NBLK))
            factor_ref[:, cols] = BETA * f_ref[:, cols] + SCALE * g_ref[:, k * BLK : (k + 1) * BLK].astype(f32)
        for k in range(1, NBLK - KEEP + 1):
            other = lax.rem(block + NBLK - k, NBLK)
            lanes = pl.ds(pl.multiple_of(k * BLK + (part // 2) * 128, 128), 128)
            slab = d_ref[block_cols(other), lanes]
            turn[...] = slab.astype(f32).T
            start = pl.multiple_of(lax.rem(part, 2) * ROWS, ROWS)
            factor_ref[:, block_cols(other)] = turn[pl.ds(start, ROWS), :]

    return call(
        kernel,
        [rows_of(f32), rows_of()],
        [VM] * 5,
        [VM] * 2,
        [pltpu.VMEM((ROWS, W), bf16), pltpu.VMEM((128, BLK), f32)],
        "refresh",
        32,
        flops=4 * ROWS * W * W,
        moved=4 * W * KW,
    )(damped_all, stale_all, stale_rows, gram_rows, factor_old)


def collect(leaving):
    def kernel(*refs):
        sources, (out_ref, sems) = refs[: len(leaving)], refs[len(leaving) :]
        section = lax.axis_index("section")
        for m in range(MICROS):
            pick(LAST - section + m, sources, out_ref.at[m], sems.at[m])
        for m in range(MICROS):
            pltpu.make_async_copy(sources[0], out_ref.at[m], sems.at[m]).wait()

    return call(
        kernel,
        jax.ShapeDtypeStruct((MICROS, ROWS, W), bf16),
        [ANY] * len(leaving),
        ANY,
        [pltpu.SemaphoreType.DMA((MICROS,))],
        "collect",
        8,
    )(*leaving)


def per_device(inputs, cotangent, weight, factor_old, stale_inverse):
    weight_mat = weight[0]
    factor_old = factor_old[0]
    stale_rows = stale_inverse[0]

    stale_all = lax.all_gather(kept_columns(stale_rows), "dp", axis=0, tiled=True)

    arriving = inputs[0]
    arrivals, slopes = [], []
    for tick in range(TICKS):
        leaving, slope = forward_tick(tick, inputs, arriving, weight_mat)
        slopes.append(slope)
        route = [(s, s + 1) for s in range(LAST) if 0 <= tick - s < MICROS]
        if tick < TICKS - 1:
            arriving = lax.ppermute(leaving, "section", route)
            arrivals.append(arriving)

    partial_gram = gram(inputs, arrivals)
    gram_xc = lax.psum_scatter(
        partial_gram, "dp", scatter_dimension=0, tiled=True, axis_index_groups=GROUP_XC
    )
    gram_rows = lax.psum_scatter(gram_xc, "dp", scatter_dimension=0, tiled=True, axis_index_groups=GROUP_Z)
    damped = damped_rows(gram_rows, factor_old)
    damped_all = lax.all_gather(damped, "dp", axis=0, tiled=True)
    factor, refined = refresh(damped_all, stale_all, stale_rows, gram_rows, factor_old)

    arriving = cotangent[0]
    leavings = []
    for tick in range(TICKS):
        leaving = backward_tick(tick, cotangent, arriving, slopes, weight_mat)
        leavings.append(leaving)
        route = [(s, s - 1) for s in range(1, SECTIONS) if 0 <= tick - (LAST - s) < MICROS]
        if tick < TICKS - 1:
            arriving = lax.ppermute(leaving, "section", route)
    grads = collect(leavings)
    return (grads[None], factor[None], refined[None])


def solution(mesh):
    placed = (
        P(None, "dp", None),
        P(None, "dp", None),
        P("section", None, None),
        P("section", "dp", None),
        P("section", "dp", None),
    )
    return jax.shard_map(
        per_device,
        mesh=mesh,
        in_specs=placed,
        out_specs=(
            P("section", None, "dp", None),
            P("section", "dp", None),
            P("section", "dp", None),
        ),
        check_vma=False,
    )
```

time: 794 us -> 500 us (0.63)
  waiting for transfers between devices: 495 us -> 360 us
  starting transfers between devices: 118 us -> 44.6 us
  matrix products: 63.2 us -> 0 us
  other arithmetic: 51.9 us -> 0 us
  Pallas kernels: 0 us -> 45.4 us
  loops' own time: 30 us -> 0 us
  local copies, waits for them, and re-layouts: 17.3 us -> 29.7 us
    all_gather x2, waiting for transfers between devices: 94.2 us -> 0.04 us  [the longest x1 0.03 us: per_device(): lax.all_gather(kept_columns(stale_rows), 'dp', axis=0, tiled=True)]
    ppermute x22 -> x20, starting transfers between devices: 118 us -> 44.5 us  [per_device(): arriving = lax.ppermute(leaving, 'section', route)]
    dot_general x11 -> x0, matrix products: 63.2 us -> none  [the longest x4 24.2 us: backward_work(): lax.dot_general(scaled, weight_mat, (((1,), (1,)), ((), ())), preferred_e...]
    select_n x44 -> x0, other arithmetic: 51.1 us -> none  [the longest x11 20.3 us: forward_tick(): jnp.where(is_valid, lax.dynamic_update_index_in_dim(stored, current, slot...]
    ppermute x22 -> x20, waiting for transfers between devices: 247 us -> 200 us  [per_device(): arriving = lax.ppermute(leaving, 'section', route)]
    pallas_call x0 -> x27, Pallas kernels: none -> 45.4 us  [the longest x11 21.2 us: backward_tick(): call(kernel, rows_of(), [ANY, VM, VM] + [ANY] * len(slopes), VM, [pltpu.V...]
    another operation x24 -> x0, loops' own time: 30 us -> none  [the longest x1 15.6 us: per_device(): lax.scan(backward_tick, back_state, jnp.arange(ticks, dtype=jnp.int32))]
    unnamed x6 -> x60, local copies, waits for them, and re-layouts: 0.01 us -> 28.7 us
  transfers between devices with their start and end apart: 25 -> 24, of which waited for: 24 -> 10; matrix products, arithmetic and copies ran while one was open for 10% -> 0% of each run, Pallas kernels for 0% -> 5%
where the time goes in v1:
time: 500 us; the launch traced here: 496 us
  waiting for transfers between devices  360 us (72%)
  Pallas kernels  45.4 us (9%)
  starting transfers between devices  44.6 us (9%)
  local copies, waits for them, and re-layouts  29.7 us (6%)
  between operations  16.4 us (3%)
    ppermute x20, waiting for transfers between devices, per_device(): arriving = lax.ppermute(leaving, 'section', route)  200 us
    reduce_scatter x1, waiting for transfers between devices, per_device(): lax.psum_scatter(partial_gram, 'dp', scatter_dimension=0, tiled=True, axi...  130 us
    ppermute x20, starting transfers between devices, per_device(): arriving = lax.ppermute(leaving, 'section', route)  44.5 us
    reduce_scatter x1, waiting for transfers between devices, per_device(): lax.psum_scatter(gram_xc, 'dp', scatter_dimension=0, tiled=True, axis_ind...  29.9 us
    unnamed x60, local copies, waits for them, and re-layouts  28.7 us
    pallas_call x11, Pallas kernels, backward_tick(): call(kernel, rows_of(), [ANY, VM, VM] + [ANY] * len(slopes), VM, [pltpu.V...  21.2 us
    pallas_call x1, Pallas kernels, gram(): call(kernel, rows_of(rows=W, cols=KW), [ANY] * (1 + len(arrivals)), ANY,...  10.9 us
  transfers between devices with their start and end apart: 24, of which 10 were waited for; matrix products, arithmetic and copies ran while one was open for 0% of the time, Pallas kernels for 5%

profile of v1, /device:TPU:64, one launch (start us, length us, event | category | flops | bytes accessed | tf_op | source)
XLA Modules:
  0.0 496.1 jit_solution(11730905896566502811)
XLA Ops:
  8.0 1.0 slice_bitcast_fusion.arriving_ref
  9.0 3.4 copy-done
  12.4 1.2 copy-done.4
  13.6 1.6 forward_tick.11
  15.3 6.0 %collective-permute-start = (bf16[64,2048]{1,0:T(8,128)(2,1)S(1)}, bf16[64,2048]{1,0:T(8,128)(2,1)S(1)}, u32[]{:S(2)}, u32[]{:S(2)}) collective-permute-start(bf16[64,2048]{1,0:T(8,128)(2,1)S(1)} %get-tuple-element.27), channel_id=1, source_target_pairs={{0,32},{1,33},{2,34},{3,35},{4,36},{5,37},{6,38},{7,39},{8,40},{9,... | collective-permute-start | bytes 786440 | tf_op jit(solution)/shard_map/ppermute | solution.py:323
  21.2 11.1 %collective-permute-done.arriving_ref.rest_0_ = bf16[64,2048]{1,0:T(8,128)(2,1)S(1)} collective-permute-done((bf16[64,2048]{1,0:T(8,128)(2,1)S(1)}, bf16[64,2048]{1,0:T(8,128)(2,1)S(1)}, u32[]{:S(2)}, u32[]{:S(2)}) %collective-permute-start) | collective-permute-done | bytes 262176 | tf_op jit(solution)/shard_map/ppermute | solution.py:323
  32.4 1.6 forward_tick.12
  34.0 8.4 %collective-permute-start.1 = (bf16[64,2048]{1,0:T(8,128)(2,1)S(1)}, bf16[64,2048]{1,0:T(8,128)(2,1)S(1)}, u32[]{:S(2)}, u32[]{:S(2)}) collective-permute-start(bf16[64,2048]{1,0:T(8,128)(2,1)S(1)} %get-tuple-element.29), channel_id=1, source_target_pairs={{0,32},{32,64},{1,33},{33,65},{2,34},{34,66},{3,35},{35,67},{4,36}... | collective-permute-start | bytes 786440 | tf_op jit(solution)/shard_map/ppermute | solution.py:323
  42.4 5.5 %collective-permute-done.1.arriving_ref.rest_1_ = bf16[64,2048]{1,0:T(8,128)(2,1)S(1)} collective-permute-done((bf16[64,2048]{1,0:T(8,128)(2,1)S(1)}, bf16[64,2048]{1,0:T(8,128)(2,1)S(1)}, u32[]{:S(2)}, u32[]{:S(2)}) %collective-permute-start.1) | collective-permute-done | bytes 262176 | tf_op jit(solution)/shard_map/ppermute | solution.py:323
  47.9 1.6 forward_tick.13
  49.5 8.3 %collective-permute-start.2 = (bf16[64,2048]{1,0:T(8,128)(2,1)S(1)}, bf16[64,2048]{1,0:T(8,128)(2,1)S(1)}, u32[]{:S(2)}, u32[]{:S(2)}) collective-permute-start(bf16[64,2048]{1,0:T(8,128)(2,1)S(1)} %get-tuple-element.31), channel_id=1, source_target_pairs={{0,32},{32,64},{64,96},{1,33},{33,65},{65,97},{2,34},{34,66},{66,9... | collective-permute-start | bytes 786440 | tf_op jit(solution)/shard_map/ppermute | solution.py:323
  57.9 4.6 collective-permute-done.2.arriving_ref.rest_2_
  62.4 1.6 forward_tick.14
  64.0 8.3 %collective-permute-start.3 = (bf16[64,2048]{1,0:T(8,128)(2,1)S(1)}, bf16[64,2048]{1,0:T(8,128)(2,1)S(1)}, u32[]{:S(2)}, u32[]{:S(2)}) collective-permute-start(bf16[64,2048]{1,0:T(8,128)(2,1)S(1)} %get-tuple-element.33), channel_id=1, source_target_pairs={{0,32},{32,64},{64,96},{96,128},{1,33},{33,65},{65,97},{97,129},{2... | collective-permute-start | bytes 786440 | tf_op jit(solution)/shard_map/ppermute | solution.py:323
  72.4 3.9 collective-permute-done.3.arriving_ref.rest_3_
  76.2 0.7 collective-permute-start.4
  77.0 0.7 copy-done.7
  77.7 0.7 collective-permute-start.5
  78.4 0.7 copy-done.9
  79.1 0.7 collective-permute-start.6
  79.8 0.7 copy-done.11
  80.5 0.7 collective-permute-start.7
  81.2 0.7 copy-done.13
  81.9 0.8 collective-permute-start.8
  83.1 0.7 copy-done.15
  83.7 0.7 collective-permute-start.9
  84.4 10.9 %gram.1 = bf16[2048,1280]{1,0:T(8,128)(2,1)S(1)} custom-call(bf16[4,64,2048]{2,1,0:T(8,128)(2,1)S(1)} %copy-done.5, bf16[64,2048]{1,0:T(8,128)(2,1)S(1)} %collective-permute-done.arriving_ref.rest_0_, bf16[64,2048]{1,0:T(8,128)(2,1)S(1)} %collective-permute-done.1.arriving_ref.rest_1_, bf16[64,2048]{1,0:T(8,128)(2,1)S(1)} %collective-permute-done.2.arriving_ref.rest_2_, ...), custom_call_target="tpu_custom_call" | custom-call | flops 1342177280 | bytes 5242880 | tf_op jit(solution)/shard_map/gram/pallas_call | solution.py:188
  95.3 2.3 copy-done.17
  97.7 0.7 copy-done.22
  98.4 129.8 %reduce-scatter.3.cloned.1.call-done = bf16[256,1280]{1,0:T(8,128)(2,1)} async-done(((bf16[2048,1280]{1,0:T(8,128)(2,1)}), bf16[256,1280]{1,0:T(8,128)(2,1)}) %reduce-scatter.3.cloned.1.call-update) | async-done | bytes 655376 | tf_op jit(solution)/shard_map/reduce_scatter | solution.py:327
  228.3 0.9 copy-done.24
  229.3 0.7 copy-done.26
  230.0 29.9 %reduce-scatter.5.cloned.1.call-done.g_ref = bf16[64,1280]{1,0:T(8,128)(2,1)} async-done(((bf16[256,1280]{1,0:T(8,128)(2,1)}), bf16[64,1280]{1,0:T(8,128)(2,1)}) %reduce-scatter.5.cloned.1.call-update) | async-done | bytes 163856 | tf_op jit(solution)/shard_map/reduce_scatter | solution.py:330
  259.9 1.1 copy-done.20
  261.0 0.9 copy-done.28
  262.0 0.7 copy-done.27
  262.7 3.5 copy-done.2
  266.2 0.9 copy-done.23
  267.2 0.7 forward_tick.21
  267.9 0.3 copy-done.12
  268.4 3.4 copy-done.3
  271.8 0.7 collective-permute-start.10
  272.6 0.7 collective-permute-start.11
  273.3 0.7 collective-permute-start.12
  274.0 9.8 %backward_tick.14.refs_3_ = bf16[64,2048]{1,0:T(8,128)(2,1)S(1)} custom-call(bf16[4,64,2048]{2,1,0:T(8,128)(2,1)S(1)} %copy-done.6, bf16[64,2048]{1,0:T(8,128)(2,1)S(1)} %collective-permute-done.12.arriving_ref, bf16[2048,2048]{1,0:T(8,128)(2,1)S(1)} %bitcast.24, bf16[64,2048]{1,0:T(8,128)(2,1)S(1)} %get-tuple-element.26.rest_0_, ...), custom_call_target="tpu_custom_call" | custom-call | flops 536870912 | bytes 8388608 | tf_op jit(solution)/shard_map/backward_tick/pallas_call | solution.py:140
  283.8 0.7 collective-permute-start.13
  284.6 0.7 collective-permute-start.14
  285.3 0.7 collective-permute-start.15
  286.0 1.3 collective-permute-start.16
  287.3 118.4 %collective-permute-done.16.arriving_ref = bf16[64,2048]{1,0:T(8,128)(2,1)S(1)} collective-permute-done((bf16[64,2048]{1,0:T(8,128)(2,1)S(1)}, bf16[64,2048]{1,0:T(8,128)(2,1)S(1)}, u32[]{:S(2)}, u32[]{:S(2)}) %collective-permute-start.16) | collective-permute-done | bytes 262176 | tf_op jit(solution)/shard_map/ppermute | solution.py:342
  405.7 2.8 backward_tick.18.refs_7_
  408.5 1.3 collective-permute-start.17
  409.8 25.2 %collective-permute-done.17.arriving_ref = bf16[64,2048]{1,0:T(8,128)(2,1)S(1)} collective-permute-done((bf16[64,2048]{1,0:T(8,128)(2,1)S(1)}, bf16[64,2048]{1,0:T(8,128)(2,1)S(1)}, u32[]{:S(2)}, u32[]{:S(2)}) %collective-permute-start.17) | collective-permute-done | bytes 262176 | tf_op jit(solution)/shard_map/ppermute | solution.py:342
  435.0 2.7 backward_tick.19.refs_8_
  437.7 1.3 collective-permute-start.18
  439.0 19.2 %collective-permute-done.18.arriving_ref = bf16[64,2048]{1,0:T(8,128)(2,1)S(1)} collective-permute-done((bf16[64,2048]{1,0:T(8,128)(2,1)S(1)}, bf16[64,2048]{1,0:T(8,128)(2,1)S(1)}, u32[]{:S(2)}, u32[]{:S(2)}) %collective-permute-start.18) | collective-permute-done | bytes 262176 | tf_op jit(solution)/shard_map/ppermute | solution.py:342
  458.2 2.7 backward_tick.20.refs_9_
  461.0 1.4 collective-permute-start.19
  462.4 12.4 %collective-permute-done.19.arriving_ref = bf16[64,2048]{1,0:T(8,128)(2,1)S(1)} collective-permute-done((bf16[64,2048]{1,0:T(8,128)(2,1)S(1)}, bf16[64,2048]{1,0:T(8,128)(2,1)S(1)}, u32[]{:S(2)}, u32[]{:S(2)}) %collective-permute-start.19) | collective-permute-done | bytes 262176 | tf_op jit(solution)/shard_map/ppermute | solution.py:342
  474.8 2.9 backward_tick.21.refs_10_
  477.7 1.0 collect.1
  478.9 2.5 copy-done.18
  481.3 2.5 copy-done.19
  483.8 4.6 refresh.1
  (77 shorter events, 1.3 us)
Async XLA Ops:
  8.0 220.2 %reduce-scatter.3.cloned.1.call-start = ((), (), s32[]{:S(2)}) async-start(), calls=%async_computation.2 | async-start | bytes 5898240 | tf_op jit(solution)/shard_map/reduce_scatter | solution.py:327
  9.0 3.4 copy-start
  12.4 1.2 copy-start.4
  13.6 18.8 %copy-start.1 = (bf16[1,2048,2048]{2,1,0:T(8,128)(2,1)S(1)}, bf16[1,2048,2048]{2,1,0:T(8,128)(2,1)}, u32[]{:S(2)}) copy-start(bf16[1,2048,2048]{2,1,0:T(8,128)(2,1)} %param.7) | copy-start | bytes 25165828
  15.3 17.1 %collective-permute-start = (bf16[64,2048]{1,0:T(8,128)(2,1)S(1)}, bf16[64,2048]{1,0:T(8,128)(2,1)S(1)}, u32[]{:S(2)}, u32[]{:S(2)}) collective-permute-start(bf16[64,2048]{1,0:T(8,128)(2,1)S(1)} %get-tuple-element.27), channel_id=1, source_target_pairs={{0,32},{1,33},{2,34},{3,35},{4,36},{5,37},{6,38},{7,39},{8,40},{9,... | collective-permute-start | bytes 786440 | tf_op jit(solution)/shard_map/ppermute | solution.py:323
  34.0 13.9 %collective-permute-start.1 = (bf16[64,2048]{1,0:T(8,128)(2,1)S(1)}, bf16[64,2048]{1,0:T(8,128)(2,1)S(1)}, u32[]{:S(2)}, u32[]{:S(2)}) collective-permute-start(bf16[64,2048]{1,0:T(8,128)(2,1)S(1)} %get-tuple-element.29), channel_id=1, source_target_pairs={{0,32},{32,64},{1,33},{33,65},{2,34},{34,66},{3,35},{35,67},{4,36}... | collective-permute-start | bytes 786440 | tf_op jit(solution)/shard_map/ppermute | solution.py:323
  49.5 12.9 %collective-permute-start.2 = (bf16[64,2048]{1,0:T(8,128)(2,1)S(1)}, bf16[64,2048]{1,0:T(8,128)(2,1)S(1)}, u32[]{:S(2)}, u32[]{:S(2)}) collective-permute-start(bf16[64,2048]{1,0:T(8,128)(2,1)S(1)} %get-tuple-element.31), channel_id=1, source_target_pairs={{0,32},{32,64},{64,96},{1,33},{33,65},{65,97},{2,34},{34,66},{66,9... | collective-permute-start | bytes 786440 | tf_op jit(solution)/shard_map/ppermute | solution.py:323
  64.0 12.2 %collective-permute-start.3 = (bf16[64,2048]{1,0:T(8,128)(2,1)S(1)}, bf16[64,2048]{1,0:T(8,128)(2,1)S(1)}, u32[]{:S(2)}, u32[]{:S(2)}) collective-permute-start(bf16[64,2048]{1,0:T(8,128)(2,1)S(1)} %get-tuple-element.33), channel_id=1, source_target_pairs={{0,32},{32,64},{64,96},{96,128},{1,33},{33,65},{65,97},{97,129},{2... | collective-permute-start | bytes 786440 | tf_op jit(solution)/shard_map/ppermute | solution.py:323
  76.2 0.7 collective-permute-start.4
  77.0 0.7 copy-start.7
  77.7 0.7 collective-permute-start.5
  78.4 0.7 copy-start.9
  79.1 0.7 collective-permute-start.6
  79.8 0.7 copy-start.11
  80.5 0.7 collective-permute-start.7
  81.2 0.7 copy-start.13
  81.9 2.5 copy-start.5
  81.9 0.8 collective-permute-start.8
  83.0 0.7 copy-start.15
  83.7 0.7 collective-permute-start.9
  95.3 2.3 copy-start.17
  97.6 0.7 copy-start.22
  98.3 164.3 %copy-start.6 = (bf16[4,64,2048]{2,1,0:T(8,128)(2,1)S(1)}, bf16[4,64,2048]{2,1,0:T(8,128)(2,1)}, u32[]{:S(2)}) copy-start(bf16[4,64,2048]{2,1,0:T(8,128)(2,1)} %cot_ref.21) | copy-start | bytes 3145732
  98.4 161.5 %reduce-scatter.5.cloned.1.call-start = ((), (), s32[]{:S(2)}) async-start(), calls=%async_computation.3 | async-start | bytes 819200 | tf_op jit(solution)/shard_map/reduce_scatter | solution.py:330
  228.2 250.5 %all-gather.5.cloned.1.call-start = ((), (), s32[]{:S(2)}) async-start(), calls=%async_computation.5 | async-start | bytes 5406720 | tf_op jit(solution)/shard_map/all_gather | solution.py:314
  228.3 1.0 copy-start.24
  229.3 0.7 copy-start.26
  230.0 248.8 %all-gather.3.cloned.1.call-start = ((), (), s32[]{:S(2)}) async-start(), calls=%async_computation.4 | async-start | bytes 5406720 | tf_op jit(solution)/shard_map/all_gather | solution.py:332
  259.9 1.1 copy-start.20
  261.0 0.9 copy-start.28
  261.9 0.7 copy-start.27
  262.6 5.2 %copy-start.8 = (bf16[64,2048]{1,0:T(8,128)(2,1)S(1)}, bf16[64,2048]{1,0:T(8,128)(2,1)}, u32[]{:S(2)}) copy-start(bf16[64,2048]{1,0:T(8,128)(2,1)} %copy-done.7) | copy-start | bytes 786436
  262.7 5.2 %copy-start.10 = (bf16[64,2048]{1,0:T(8,128)(2,1)S(1)}, bf16[64,2048]{1,0:T(8,128)(2,1)}, u32[]{:S(2)}) copy-start(bf16[64,2048]{1,0:T(8,128)(2,1)} %copy-done.9) | copy-start | bytes 786436
  262.7 3.5 copy-start.2
  266.2 0.9 copy-start.23
  267.2 1.0 copy-start.12
  267.2 1.1 copy-start.14
  267.2 1.2 copy-start.16
  268.4 3.4 copy-start.3
  271.8 0.7 collective-permute-start.10
  272.6 0.7 collective-permute-start.11
  273.3 0.7 collective-permute-start.12
  283.8 0.7 collective-permute-start.13
  284.6 0.7 collective-permute-start.14
  285.3 0.7 collective-permute-start.15
  286.0 119.7 %collective-permute-start.16 = (bf16[64,2048]{1,0:T(8,128)(2,1)S(1)}, bf16[64,2048]{1,0:T(8,128)(2,1)S(1)}, u32[]{:S(2)}, u32[]{:S(2)}) collective-permute-start(bf16[64,2048]{1,0:T(8,128)(2,1)S(1)} %backward_tick.17.refs_6_), channel_id=1, source_target_pairs={{32,0},{64,32},{96,64},{128,96},{33,1},{65,33},{97,65},{129,97},{3... | collective-permute-start | bytes 786440 | tf_op jit(solution)/shard_map/ppermute | solution.py:342
  408.5 26.5 %collective-permute-start.17 = (bf16[64,2048]{1,0:T(8,128)(2,1)S(1)}, bf16[64,2048]{1,0:T(8,128)(2,1)S(1)}, u32[]{:S(2)}, u32[]{:S(2)}) collective-permute-start(bf16[64,2048]{1,0:T(8,128)(2,1)S(1)} %backward_tick.18.refs_7_), channel_id=1, source_target_pairs={{32,0},{64,32},{96,64},{33,1},{65,33},{97,65},{34,2},{66,34},{98,6... | collective-permute-start | bytes 786440 | tf_op jit(solution)/shard_map/ppermute | solution.py:342
  437.7 20.5 %collective-permute-start.18 = (bf16[64,2048]{1,0:T(8,128)(2,1)S(1)}, bf16[64,2048]{1,0:T(8,128)(2,1)S(1)}, u32[]{:S(2)}, u32[]{:S(2)}) collective-permute-start(bf16[64,2048]{1,0:T(8,128)(2,1)S(1)} %backward_tick.19.refs_8_), channel_id=1, source_target_pairs={{32,0},{64,32},{33,1},{65,33},{34,2},{66,34},{35,3},{67,35},{36,4}... | collective-permute-start | bytes 786440 | tf_op jit(solution)/shard_map/ppermute | solution.py:342
  460.9 17.9 %copy-start.21 = (f32[1,64,2048]{2,1,0:T(8,128)S(1)}, f32[1,64,2048]{2,1,0:T(8,128)}, u32[]{:S(2)}) copy-start(f32[1,64,2048]{2,1,0:T(8,128)} %param.8) | copy-start | bytes 1572868
  461.0 17.9 %copy-start.25 = (bf16[1,64,2048]{2,1,0:T(8,128)(2,1)S(1)}, bf16[1,64,2048]{2,1,0:T(8,128)(2,1)}, u32[]{:S(2)}) copy-start(bf16[1,64,2048]{2,1,0:T(8,128)(2,1)} %param.9) | copy-start | bytes 786436
  461.0 17.9 %copy-start.29 = (bf16[64,1280]{1,0:T(8,128)(2,1)S(1)}, bf16[64,1280]{1,0:T(8,128)(2,1)}, u32[]{:S(2)}) copy-start(bf16[64,1280]{1,0:T(8,128)(2,1)} %reduce-scatter.5.cloned.1.call-done.g_ref) | copy-start | bytes 491524
  461.0 13.8 %collective-permute-start.19 = (bf16[64,2048]{1,0:T(8,128)(2,1)S(1)}, bf16[64,2048]{1,0:T(8,128)(2,1)S(1)}, u32[]{:S(2)}, u32[]{:S(2)}) collective-permute-start(bf16[64,2048]{1,0:T(8,128)(2,1)S(1)} %backward_tick.20.refs_9_), channel_id=1, source_target_pairs={{32,0},{33,1},{34,2},{35,3},{36,4},{37,5},{38,6},{39,7},{40,8},{41... | collective-permute-start | bytes 786440 | tf_op jit(solution)/shard_map/ppermute | solution.py:342
  478.8 2.5 copy-start.18
  481.3 2.5 copy-start.19
Sparse Core Ops, SparseCore 0:
  98.5 129.6 reduce-scatter.2
  230.8 29.0 reduce-scatter.4
Sparse Core Ops, SparseCore 1:
  230.6 69.3 all-gather.4
  301.7 83.6 all-gather.2
